TPU v7x, 512 devices: a whole 4x8x8 slice. The times are simulated.
512 devices in a mesh: snd: 64 (over y, z), rcv: 8 (over x, core).
Axes of the slice: x: 4, y: 8, z: 8, core: 2. Of those that a mesh axis runs over, the one named last changes fastest.
Arguments:
- tile_counts: bfloat16 [64, 8, 32, 256, 256], P('snd', 'rcv'), may hold values from 0 to 10, as said below
- tile_sender: int32 [64, 8, 32], P('snd', 'rcv'), may hold values from 0 to 3
- tile_receiver: int32 [64, 8, 32], P('snd', 'rcv'), may hold values from 0 to 31
- tile_action: int32 [64, 8, 32], P('snd', 'rcv'), may hold values from 0 to 255
- tile_fill: int32 [64, 8], P('snd', 'rcv'), may hold values from 1 to 32, as said below
- sender_log_shape: float32 [64, 96, 1024], P('snd', None, 'rcv'), may hold values from -0.5 to 3
- sender_log_rate: float32 [64, 96, 1024], P('snd', None, 'rcv')
- receiver_log_shape: float32 [8, 96, 8192], P('rcv', None, 'snd'), may hold values from -0.5 to 3
- receiver_log_rate: float32 [8, 96, 8192], P('rcv', None, 'snd')
- action_log_shape: float32 [96, 256], replicated, may hold values from -0.5 to 3
- action_log_rate: float32 [96, 256], replicated
Outputs:
- new_sender_log_shape: float32 [64, 96, 1024], P('snd', None, 'rcv')
- new_sender_log_rate: float32 [64, 96, 1024], P('snd', None, 'rcv')
- new_receiver_log_shape: float32 [8, 96, 8192], P('rcv', None, 'snd')
- new_receiver_log_rate: float32 [8, 96, 8192], P('rcv', None, 'snd')
- new_action_log_shape: float32 [96, 256], replicated
- new_action_log_rate: float32 [96, 256], replicated
Inputs may be any that keep to these rules, and one draw needn't show every extreme that they name: tile_fill[p, q] is the number of live slots of that device, its first slots; slots beyond it are ignored. In every draw some device has all 32 slots live. `tile_counts`: non-negative weighted counts; many entries are zero.
All inputs are finite; a program needn't handle non-finite values.
Results may differ from a plain program's by a relative error of at most 0.004.
Values may be sent and summed in bfloat16 or wider, within the bound.
A program may use at most 64 MiB of HBM per device.

v0:
```python
import jax
import jax.numpy as jnp
from jax import lax
from jax.sharding import PartitionSpec as P

prior_shape = 0.3
prior_rate = 0.3
step_size = 0.5
tile_group = 4


def digamma_series(value):
    shift_sum = jnp.zeros_like(value)
    for offset in range(6):
        shift_sum = shift_sum + 1.0 / (value + float(offset))
    moved = value + 6.0
    inverse = 1.0 / moved
    inv_square = inverse * inverse
    series = (
        jnp.log(moved)
        - 0.5 * inverse
        - inv_square * (1.0 / 12.0 - inv_square * (1.0 / 120.0 - inv_square / 252.0))
    )
    return series - shift_sum


def geometric(log_shape, log_rate):
    return jnp.exp(digamma_series(jnp.exp(log_shape)) - log_rate)


def refresh(log_value, target):
    return jnp.log((1.0 - step_size) * jnp.exp(log_value) + step_size * target)


def add_columns(running, addend, start_col):
    span_cols = addend.shape[1]
    current = lax.dynamic_slice_in_dim(running, start_col, span_cols, 1)
    return lax.dynamic_update_slice_in_dim(running, current + addend, start_col, 1)


def per_device(
    tile_counts,
    tile_sender,
    tile_receiver,
    tile_action,
    tile_fill,
    sender_log_shape,
    sender_log_rate,
    receiver_log_shape,
    receiver_log_rate,
    action_log_shape,
    action_log_rate,
):
    counts = tile_counts[0, 0]
    senders = tile_sender[0, 0]
    receivers = tile_receiver[0, 0]
    actions = tile_action[0, 0]
    live_count = tile_fill[0, 0]
    tile_edge = counts.shape[1]
    own_send_shape = sender_log_shape[0]
    own_send_rate = sender_log_rate[0]
    own_recv_shape = receiver_log_shape[0]
    own_recv_rate = receiver_log_rate[0]
    group_shape, group_rate = (
        lax.all_gather(own_send_shape, "rcv", axis=1, tiled=True),
        lax.all_gather(own_send_rate, "rcv", axis=1, tiled=True),
    )
    sender_geo = geometric(group_shape, group_rate).astype(jnp.bfloat16)
    group_shape, group_rate = (
        lax.all_gather(own_recv_shape, "snd", axis=1, tiled=True),
        lax.all_gather(own_recv_rate, "snd", axis=1, tiled=True),
    )
    receiver_geo = geometric(group_shape, group_rate).astype(jnp.bfloat16)
    sender_part = jnp.sum(jnp.exp(own_send_shape - own_send_rate), axis=1)
    receiver_part = jnp.sum(jnp.exp(own_recv_shape - own_recv_rate), axis=1)
    sender_total, receiver_total = lax.psum((sender_part, receiver_part), ("snd", "rcv"))
    action_geo = geometric(action_log_shape, action_log_rate)
    factor_rank = action_geo.shape[0]

    def one_turn(turn_index, totals):
        send_term, recv_term, act_term = totals
        first_slot = turn_index * tile_group
        slot_ids = first_slot + jnp.arange(tile_group, dtype=jnp.int32)
        live_flags = (slot_ids < live_count).astype(jnp.float32)
        block_counts = lax.dynamic_slice_in_dim(counts, first_slot, tile_group, 0)
        send_starts = [senders[first_slot + offset] * tile_edge for offset in range(tile_group)]
        recv_starts = [receivers[first_slot + offset] * tile_edge for offset in range(tile_group)]
        action_ids = [actions[first_slot + offset] for offset in range(tile_group)]
        send_blocks = jnp.stack(
            [
                lax.dynamic_slice_in_dim(sender_geo, start_col, tile_edge, 1)
                for start_col in send_starts
            ]
        )
        recv_blocks = jnp.stack(
            [
                lax.dynamic_slice_in_dim(receiver_geo, start_col, tile_edge, 1)
                for start_col in recv_starts
            ]
        )
        weights = jnp.stack(
            [lax.dynamic_slice_in_dim(action_geo, action_id, 1, 1) for action_id in action_ids]
        )
        scaled = (send_blocks.astype(jnp.float32) * weights).astype(jnp.bfloat16)
        expected = jnp.einsum(
            "tki,tkj->tij", scaled, recv_blocks, preferred_element_type=jnp.float32
        )
        ratios = (block_counts.astype(jnp.float32) * live_flags[:, None, None] / expected).astype(
            jnp.bfloat16
        )
        toward_send = jnp.einsum(
            "tkj,tij->tki", recv_blocks, ratios, preferred_element_type=jnp.float32
        )
        toward_recv = jnp.einsum("tki,tij->tkj", scaled, ratios, preferred_element_type=jnp.float32)
        send_part = scaled.astype(jnp.float32) * toward_send
        recv_part = recv_blocks.astype(jnp.float32) * toward_recv
        act_part = jnp.sum(send_part, axis=2)
        for offset in range(tile_group):
            send_term = add_columns(send_term, send_part[offset], send_starts[offset])
            recv_term = add_columns(recv_term, recv_part[offset], recv_starts[offset])
            act_term = add_columns(act_term, act_part[offset][:, None], action_ids[offset])
        return (send_term, recv_term, act_term)

    turns_needed = (live_count + tile_group - 1) // tile_group
    initial = (
        jnp.zeros((factor_rank, sender_geo.shape[1]), jnp.float32),
        jnp.zeros((factor_rank, receiver_geo.shape[1]), jnp.float32),
        jnp.zeros((factor_rank, action_geo.shape[1]), jnp.float32),
    )
    send_term, recv_term, act_term = lax.fori_loop(0, turns_needed, one_turn, initial)
    sender_stat = lax.psum_scatter(
        send_term.astype(jnp.bfloat16), "rcv", scatter_dimension=1, tiled=True
    ).astype(jnp.float32)
    receiver_stat = lax.psum_scatter(recv_term, "snd", scatter_dimension=1, tiled=True)
    action_stat = lax.psum(act_term, ("snd", "rcv"))
    action_total = jnp.sum(jnp.exp(action_log_shape - action_log_rate), axis=1)
    new_send_shape = refresh(own_send_shape, prior_shape + sender_stat)
    new_send_rate = refresh(own_send_rate, (prior_rate + receiver_total * action_total)[:, None])
    new_recv_shape = refresh(own_recv_shape, prior_shape + receiver_stat)
    new_recv_rate = refresh(own_recv_rate, (prior_rate + sender_total * action_total)[:, None])
    new_act_shape = refresh(action_log_shape, prior_shape + action_stat)
    new_act_rate = refresh(action_log_rate, (prior_rate + sender_total * receiver_total)[:, None])
    return (
        new_send_shape[None],
        new_send_rate[None],
        new_recv_shape[None],
        new_recv_rate[None],
        new_act_shape,
        new_act_rate,
    )


def solution(mesh):
    return jax.shard_map(
        per_device,
        mesh=mesh,
        in_specs=(
            P("snd", "rcv", None, None, None),
            P("snd", "rcv", None),
            P("snd", "rcv", None),
            P("snd", "rcv", None),
            P("snd", "rcv"),
            P("snd", None, "rcv"),
            P("snd", None, "rcv"),
            P("rcv", None, "snd"),
            P("rcv", None, "snd"),
            P(),
            P(),
        ),
        out_specs=(
            P("snd", None, "rcv"),
            P("snd", None, "rcv"),
            P("rcv", None, "snd"),
            P("rcv", None, "snd"),
            P(),
            P(),
        ),
        check_vma=False,
    )
```

profile of v0, /device:TPU:2, one launch (start us, length us, event | category | flops | bytes accessed | tf_op | source)
XLA Modules:
  0.0 1044.4 jit_solution(684271220119446146)
XLA Ops:
  11.3 106.2 %all-reduce = (f32[96]{0:T(128)S(1)}, f32[96]{0:T(128)S(1)}) all-reduce(f32[96]{0:T(128)S(1)} %exponential_reduce_fusion.2, f32[96]{0:T(128)S(1)} %exponential_reduce_fusion.1), channel_id=1, replica_groups=mesh['snd'=64,'rcv'=8] {'snd','rcv'}, use_global_device_ids=true, to_apply=%region_5.6 | all-reduce | flops 192 | bytes 1536 | tf_op jit(solution)/shard_map/psum | solution.py:76
  118.1 2.4 exponential_reduce_fusion
  121.2 12.0 %all-gather = f32[1,96,1024]{2,1,0:T(8,128)S(1)} all-gather(f32[1,96,128]{2,1,0:T(8,128)} %param.18), channel_id=2, replica_groups=mesh['snd'=64,'rcv'=8] {'rcv'}, dimensions={2}, use_global_device_ids=true | all-gather | bytes 442368 | tf_op jit(solution)/shard_map/all_gather | solution.py:65
  133.2 13.2 %all-gather.1 = f32[1,96,1024]{2,1,0:T(8,128)S(1)} all-gather(f32[1,96,128]{2,1,0:T(8,128)} %param.19), channel_id=3, replica_groups=mesh['snd'=64,'rcv'=8] {'rcv'}, dimensions={2}, use_global_device_ids=true | all-gather | bytes 442368 | tf_op jit(solution)/shard_map/all_gather | solution.py:66
  146.4 1.2 fusion.31
  147.6 42.8 %all-gather.9.cloned.1.call-done = f32[1,96,8192]{2,1,0:T(8,128)} async-done(((f32[1,96,128]{2,1,0:T(8,128)}), f32[1,96,8192]{2,1,0:T(8,128)}) %all-gather.9.cloned.1.call-update) | async-done | bytes 3145744 | tf_op jit(solution)/shard_map/all_gather | solution.py:71
  190.4 7.1 fusion.26
  198.5 112.3 %while.16 = (s32[]{:T(128)}, f32[96,1024]{1,0:T(8,128)S(1)}, f32[96,8192]{1,0:T(8,128)S(1)}, f32[96,256]{0,1:T(8,128)}, s32[]{:T(128)}, /*index=5*/s32[32]{0:T(1...) while((s32[]{:T(128)}, f32[96,1024]{1,0:T(8,128)S(1)}, ...), condition=%wide.region_2.0_spmd, body=%wide.region_0.2_spmd.sunk | while | flops 155387072 | bytes 7230145 | solution.py:130
  215.9 1.5 fusion.72
  217.4 1.0 convolution_multiply_fusion.3
  218.5 1.0 fusion.73
  219.5 1.2 fusion.81
  220.7 1.3 dynamic_update_slice.98
  222.0 1.2 fusion.82
  223.2 1.3 dynamic_update_slice.99
  224.5 1.2 fusion.83
  225.7 1.3 dynamic_update_slice.100
  227.0 1.2 fusion.84
  228.2 1.3 dynamic_update_slice.101
  253.3 1.5 fusion.72
  254.8 1.0 convolution_multiply_fusion.3
  255.9 1.0 fusion.73
  256.9 1.2 fusion.81
  258.1 1.3 dynamic_update_slice.98
  259.4 1.2 fusion.82
  260.6 1.3 dynamic_update_slice.99
  261.9 1.2 fusion.83
  263.1 1.3 dynamic_update_slice.100
  264.3 1.2 fusion.84
  265.5 1.3 dynamic_update_slice.101
  290.7 1.5 fusion.72
  292.2 1.0 convolution_multiply_fusion.3
  293.3 1.0 fusion.73
  294.3 1.2 fusion.81
  295.5 1.3 dynamic_update_slice.98
  296.8 1.2 fusion.82
  298.0 1.3 dynamic_update_slice.99
  299.3 1.2 fusion.83
  300.5 1.3 dynamic_update_slice.100
  301.7 1.2 fusion.84
  302.9 1.3 dynamic_update_slice.101
  310.8 1.9 copy.20
  313.5 1.8 copy.21
  317.4 434.7 %all-reduce.3.cloned.1.call-done = f32[96,256]{1,0:T(8,128)} async-done(((f32[96,256]{1,0:T(8,128)}), f32[96,256]{1,0:T(8,128)}) %all-reduce.3.cloned.1.call-update) | async-done | bytes 98320 | tf_op jit(solution)/shard_map/psum | solution.py:135
  752.1 1.6 multiply_log_fusion
  753.6 30.6 %reduce-scatter.7.cloned.1.call-done = bf16[128,96]{1,0:T(8,128)(2,1)} async-done(((bf16[1024,96]{1,0:T(8,128)(2,1)}), bf16[128,96]{1,0:T(8,128)(2,1)}) %reduce-scatter.7.cloned.1.call-update) | async-done | bytes 24592
  785.7 250.7 %reduce-scatter.5.cloned.1.call-done = f32[96,128]{1,0:T(8,128)} async-done(((f32[96,8192]{1,0:T(8,128)}), f32[96,128]{1,0:T(8,128)}) %reduce-scatter.5.cloned.1.call-update) | async-done | bytes 49168 | tf_op jit(solution)/shard_map/reduce_scatter | solution.py:134
  1036.4 1.4 fusion.37
  (97 shorter events, 44.7 us)
Async XLA Ops:
  7.2 140.4 %all-gather.7.cloned.1.call-start = ((), (), s32[]{:S(2)}) async-start(), calls=%async_computation.4 | async-start | bytes 3194880 | tf_op jit(solution)/shard_map/all_gather | solution.py:70
  7.9 182.5 %all-gather.9.cloned.1.call-start = ((), (), s32[]{:S(2)}) async-start(), calls=%async_computation.5 | async-start | bytes 3194880 | tf_op jit(solution)/shard_map/all_gather | solution.py:71
  8.7 743.4 %all-reduce.3.cloned.1.call-start = ((), (), s32[]{:S(2)}) async-start(), calls=%async_computation.3 | async-start | bytes 196608 | tf_op jit(solution)/shard_map/psum | solution.py:135
  117.5 0.6 copy-start.10
  117.5 0.6 copy-start.12
  197.5 1.0 copy-start.6
  197.5 1.0 copy-start.7
  197.5 1.0 copy-start.8
  310.8 4.6 copy-start
  310.8 5.1 copy-start.9
  310.8 5.1 copy-start.11
  310.8 5.1 copy-start.13
  312.7 471.5 %reduce-scatter.7.cloned.1.call-start = ((), (), s32[]{:S(2)}) async-start(), calls=%async_computation.6 | async-start | bytes 294912
  313.4 2.5 copy-start.1
  313.4 3.2 copy-start.2
  313.4 438.6 %copy-start.5 = (f32[96,256]{1,0:T(8,128)S(1)}, f32[96,256]{1,0:T(8,128)}, u32[]{:S(2)}) copy-start(f32[96,256]{1,0:T(8,128)} %param.22) | copy-start | bytes 294916
  313.4 471.6 %copy-start.3 = (f32[1,96,128]{2,1,0:T(8,128)S(1)}, f32[1,96,128]{2,1,0:T(8,128)}, u32[]{:S(2)}) copy-start(f32[1,96,128]{2,1,0:T(8,128)} %param.18) | copy-start | bytes 147460
  313.5 722.9 %copy-start.4 = (f32[1,96,128]{2,1,0:T(8,128)S(1)}, f32[1,96,128]{2,1,0:T(8,128)}, u32[]{:S(2)}) copy-start(f32[1,96,128]{2,1,0:T(8,128)} %param.20) | copy-start | bytes 147460
  315.3 721.1 %reduce-scatter.5.cloned.1.call-start = ((), (), s32[]{:S(2)}) async-start(), calls=%async_computation.2 | async-start | bytes 3194880 | tf_op jit(solution)/shard_map/reduce_scatter | solution.py:134
Sparse Core Ops, SparseCore 0:
  11.0 92.6 all-gather.6
  106.6 83.6 all-gather.8
  312.8 439.2 all-reduce.2
  754.9 29.2 reduce-scatter.6
  788.1 248.2 reduce-scatter.4
where the time goes:
time: 1050 us; the launch traced here: 1040 us
  waiting for transfers between devices  761 us (72%)
  blocking collectives  131 us (12%)
  other arithmetic  54.1 us (5%)
  loops' own time  37 us (4%)
  local copies, waits for them, and re-layouts  35.5 us (3%)
  between operations  14.6 us (1%)
  matrix products  10.8 us (1%)
    psum x1, waiting for transfers between devices, per_device(): action_stat = lax.psum(act_term, ('snd', 'rcv'))  435 us
    reduce_scatter x1, waiting for transfers between devices, per_device(): lax.psum_scatter(recv_term, 'snd', scatter_dimension=1, tiled=True)  251 us
    psum x1, blocking collectives, per_device(): lax.psum((sender_part, receiver_part), ('snd', 'rcv'))  106 us
    all_gather x1, waiting for transfers between devices, per_device(): lax.all_gather(own_recv_rate, 'snd', axis=1, tiled=True)  42.8 us
    another operation x1, loops' own time, per_device(): lax.fori_loop(0, turns_needed, one_turn, initial)  37 us
    unnamed x6, waiting for transfers between devices  32.5 us
  transfers between devices with their start and end apart: 5, of which 4 were waited for; matrix products, arithmetic and copies ran while one was open for 1% of the time, Pallas kernels for 0%

commit v1 on v0

--- a/solution.py
+++ b/solution.py
@@ -132,7 +132,7 @@
         send_term.astype(jnp.bfloat16), "rcv", scatter_dimension=1, tiled=True
     ).astype(jnp.float32)
     receiver_stat = lax.psum_scatter(recv_term, "snd", scatter_dimension=1, tiled=True)
-    action_stat = lax.psum(act_term, ("snd", "rcv"))
+    action_stat = jnp.sum(lax.all_gather(act_term, ("snd", "rcv")), axis=0)
     action_total = jnp.sum(jnp.exp(action_log_shape - action_log_rate), axis=1)
     new_send_shape = refresh(own_send_shape, prior_shape + sender_stat)
     new_send_rate = refresh(own_send_rate, (prior_rate + receiver_total * action_total)[:, None])

time: 1050 us -> 961 us (0.915)
  the two profiles are of different devices: /device:TPU:2 before, /device:TPU:1 now
where the time goes in v1:
time: 961 us; the launch traced here: 956 us
  waiting for transfers between devices  636 us (66%)
  blocking collectives  135 us (14%)
  other arithmetic  59 us (6%)
  loops' own time  51.2 us (5%)
  local copies, waits for them, and re-layouts  50.3 us (5%)
  between operations  14.6 us (2%)
  matrix products  9.62 us (1%)
    reduce_scatter x1, waiting for transfers between devices, per_device(): lax.psum_scatter(recv_term, 'snd', scatter_dimension=1, tiled=True)  245 us
    all_gather x1, waiting for transfers between devices, per_device(): action_stat = jnp.sum(lax.all_gather(act_term, ('snd', 'rcv')), axis=0)  196 us
    unnamed x6, waiting for transfers between devices  160 us
    psum x1, blocking collectives, per_device(): lax.psum((sender_part, receiver_part), ('snd', 'rcv'))  107 us
    another operation x1, loops' own time, per_device(): lax.fori_loop(0, turns_needed, one_turn, initial)  51.2 us
    all_gather x1, waiting for transfers between devices, per_device(): lax.all_gather(own_recv_shape, 'snd', axis=1, tiled=True)  35.9 us
    dynamic_update_slice x16, local copies, waits for them, and re-layouts, add_columns(): lax.dynamic_update_slice_in_dim(running, current + addend, start_col, 1)  20.5 us
  transfers between devices with their start and end apart: 5, of which 4 were waited for; matrix products, arithmetic and copies ran while one was open for 1% of the time, Pallas kernels for 0%

profile of v1, /device:TPU:1, one launch (start us, length us, event | category | flops | bytes accessed | tf_op | source)
XLA Modules:
  0.0 955.8 jit_solution(14767904017831828997)
XLA Ops:
  11.3 106.9 %all-reduce = (f32[96]{0:T(128)S(1)}, f32[96]{0:T(128)S(1)}) all-reduce(f32[96]{0:T(128)S(1)} %exponential_reduce_fusion.2, f32[96]{0:T(128)S(1)} %exponential_reduce_fusion.1), channel_id=1, replica_groups=mesh['snd'=64,'rcv'=8] {'snd','rcv'}, use_global_device_ids=true, to_apply=%region_5.6 | all-reduce | flops 192 | bytes 1536 | tf_op jit(solution)/shard_map/psum | solution.py:76
  118.6 2.5 exponential_reduce_fusion
  121.8 14.7 %all-gather.1 = f32[1,96,1024]{2,1,0:T(8,128)S(1)} all-gather(f32[1,96,128]{2,1,0:T(8,128)} %param.19), channel_id=3, replica_groups=mesh['snd'=64,'rcv'=8] {'rcv'}, dimensions={2}, use_global_device_ids=true | all-gather | bytes 442368 | tf_op jit(solution)/shard_map/all_gather | solution.py:66
  136.6 13.2 %all-gather = f32[1,96,1024]{2,1,0:T(8,128)S(1)} all-gather(f32[1,96,128]{2,1,0:T(8,128)} %param.18), channel_id=2, replica_groups=mesh['snd'=64,'rcv'=8] {'rcv'}, dimensions={2}, use_global_device_ids=true | all-gather | bytes 442368 | tf_op jit(solution)/shard_map/all_gather | solution.py:65
  149.7 1.3 fusion.31
  151.0 35.9 %all-gather.9.cloned.1.call-done = f32[1,96,8192]{2,1,0:T(8,128)} async-done(((f32[1,96,128]{2,1,0:T(8,128)}), f32[1,96,8192]{2,1,0:T(8,128)}) %all-gather.9.cloned.1.call-update) | async-done | bytes 3145744 | tf_op jit(solution)/shard_map/all_gather | solution.py:70
  186.9 7.1 fusion.26
  194.9 127.6 %while.16 = (s32[]{:T(128)}, f32[96,1024]{1,0:T(8,128)S(1)}, f32[96,8192]{1,0:T(8,128)S(1)}, f32[96,256]{0,1:T(8,128)}, s32[]{:T(128)}, /*index=5*/s32[32]{0:T(1...) while((s32[]{:T(128)}, f32[96,1024]{1,0:T(8,128)S(1)}, ...), condition=%wide.region_2.0_spmd, body=%wide.region_0.2_spmd.sunk | while | flops 155387072 | bytes 8803241 | solution.py:130
  198.9 1.6 dynamic-slice_bitcast_fusion.10
  203.7 1.6 dynamic-slice_bitcast_fusion.11
  214.2 1.8 fusion.72
  216.9 1.2 fusion.81
  218.1 1.3 dynamic_update_slice.98
  220.6 1.3 dynamic_update_slice.99
  223.1 1.3 dynamic_update_slice.100
  225.5 1.3 dynamic_update_slice.101
  230.7 1.6 dynamic-slice_bitcast_fusion.10
  235.5 1.6 dynamic-slice_bitcast_fusion.11
  246.0 1.8 fusion.72
  248.7 1.2 fusion.81
  249.9 1.3 dynamic_update_slice.98
  252.4 1.3 dynamic_update_slice.99
  253.7 1.2 fusion.83
  254.9 1.3 dynamic_update_slice.100
  256.2 1.2 fusion.84
  257.4 1.3 dynamic_update_slice.101
  262.5 1.6 dynamic-slice_bitcast_fusion.10
  267.4 1.7 dynamic-slice_bitcast_fusion.11
  277.9 1.8 fusion.72
  280.7 1.2 fusion.81
  281.9 1.3 dynamic_update_slice.98
  284.4 1.3 dynamic_update_slice.99
  286.8 1.3 dynamic_update_slice.100
  289.3 1.3 dynamic_update_slice.101
  294.5 1.6 dynamic-slice_bitcast_fusion.10
  299.3 1.7 dynamic-slice_bitcast_fusion.11
  309.9 1.8 fusion.72
  313.8 1.3 dynamic_update_slice.98
  315.1 1.2 fusion.82
  316.3 1.3 dynamic_update_slice.99
  318.8 1.3 dynamic_update_slice.100
  321.2 1.3 dynamic_update_slice.101
  323.3 2.2 copy.22
  328.4 158.1 %reduce-scatter.7.cloned.1.call-done = bf16[128,96]{1,0:T(8,128)(2,1)} async-done(((bf16[1024,96]{1,0:T(8,128)(2,1)}), bf16[128,96]{1,0:T(8,128)(2,1)}) %reduce-scatter.7.cloned.1.call-update) | async-done | bytes 24592
  488.0 244.7 %reduce-scatter.5.cloned.1.call-done = f32[96,128]{1,0:T(8,128)} async-done(((f32[96,8192]{1,0:T(8,128)}), f32[96,128]{1,0:T(8,128)}) %reduce-scatter.5.cloned.1.call-update) | async-done | bytes 49168 | tf_op jit(solution)/shard_map/reduce_scatter | solution.py:134
  732.7 1.4 fusion.37
  734.2 195.5 %all-gather.13.cloned.1.call-done = f32[49152,256]{1,0:T(8,128)} async-done(((f32[96,256]{1,0:T(8,128)}), f32[49152,256]{1,0:T(8,128)}) %all-gather.13.cloned.1.call-update) | async-done | bytes 50331664 | tf_op jit(solution)/shard_map/all_gather | solution.py:135
  929.7 18.9 %reduce_sum.51 = f32[96,256]{1,0:T(8,128)S(1)} reduce(f32[512,96,256]{2,1,0:T(8,128)} %bitcast.238, f32[]{:T(128)} %constant.128.clone.1), dimensions={0}, to_apply=%region_10.11 | reduce | flops 12558336 | bytes 50429956 | tf_op jit(solution)/shard_map/reduce_sum | solution.py:135
  (190 shorter events, 40.4 us)
Async XLA Ops:
  7.2 143.8 %all-gather.11.cloned.1.call-start = ((), (), s32[]{:S(2)}) async-start(), calls=%async_computation.4 | async-start | bytes 3194880 | tf_op jit(solution)/shard_map/all_gather | solution.py:71
  7.9 179.0 %all-gather.9.cloned.1.call-start = ((), (), s32[]{:S(2)}) async-start(), calls=%async_computation.3 | async-start | bytes 3194880 | tf_op jit(solution)/shard_map/all_gather | solution.py:70
  8.6 477.8 %reduce-scatter.7.cloned.1.call-start = ((), (), s32[]{:S(2)}) async-start(), calls=%async_computation.6 | async-start | bytes 294912
  194.0 1.0 copy-start.17
  213.3 2.7 copy-start.1
  213.3 2.7 copy-start.2
  213.3 2.7 copy-start.3
  213.3 2.7 copy-start.4
  213.3 2.7 copy-start.5
  213.3 2.6 copy-start.6
  213.4 2.6 copy-start.7
  213.4 2.6 copy-start.8
  245.1 2.7 copy-start.1
  245.1 2.7 copy-start.2
  245.1 2.7 copy-start.3
  245.1 2.7 copy-start.4
  245.1 2.7 copy-start.5
  245.2 2.6 copy-start.6
  245.2 2.6 copy-start.7
  245.2 2.6 copy-start.8
  277.1 2.7 copy-start.1
  277.1 2.7 copy-start.2
  277.1 2.7 copy-start.3
  277.1 2.7 copy-start.4
  277.1 2.6 copy-start.5
  277.1 2.6 copy-start.6
  277.1 2.6 copy-start.7
  277.1 2.6 copy-start.8
  309.0 2.7 copy-start.1
  309.0 2.7 copy-start.2
  309.0 2.7 copy-start.3
  309.0 2.7 copy-start.4
  309.0 2.6 copy-start.5
  309.0 2.6 copy-start.6
  309.0 2.6 copy-start.7
  309.1 2.6 copy-start.8
  322.5 3.1 copy-start
  322.5 4.4 copy-start.18
  322.5 4.4 copy-start.20
  322.5 4.4 copy-start.22
  323.3 2.9 copy-start.9
  323.3 3.7 copy-start.10
  323.3 4.4 copy-start.11
  323.3 164.0 %copy-start.12 = (f32[1,96,128]{2,1,0:T(8,128)S(1)}, f32[1,96,128]{2,1,0:T(8,128)}, u32[]{:S(2)}) copy-start(f32[1,96,128]{2,1,0:T(8,128)} %param.18) | copy-start | bytes 147460
  323.3 409.4 %copy-start.13 = (f32[1,96,128]{2,1,0:T(8,128)S(1)}, f32[1,96,128]{2,1,0:T(8,128)}, u32[]{:S(2)}) copy-start(f32[1,96,128]{2,1,0:T(8,128)} %param.20) | copy-start | bytes 147460
  325.5 407.2 %reduce-scatter.5.cloned.1.call-start = ((), (), s32[]{:S(2)}) async-start(), calls=%async_computation.2 | async-start | bytes 3194880 | tf_op jit(solution)/shard_map/reduce_scatter | solution.py:134
  326.1 603.6 %all-gather.13.cloned.1.call-start = ((), (), s32[]{:S(2)}) async-start(), calls=%async_computation.5 | async-start | bytes 50429952 | tf_op jit(solution)/shard_map/all_gather | solution.py:135
  929.7 18.9 %copy-start.14 = (f32[96,256]{1,0:T(8,128)S(1)}, f32[96,256]{1,0:T(8,128)}, u32[]{:S(2)}) copy-start(f32[96,256]{1,0:T(8,128)} %param.22) | copy-start | bytes 294916
  (4 other events, 3.0 us)
Sparse Core Ops, SparseCore 0:
  11.0 89.3 all-gather.10
  103.4 83.4 all-gather.8
  325.6 160.7 reduce-scatter.6
  491.0 241.7 reduce-scatter.4
  738.4 191.2 all-gather.12
